TPU v7x, 32 devices: a whole 2x2x4 slice. The times are simulated.
32 devices in a mesh: elem: 2 (over x), band: 16 (over z, y, core).
Axes of the slice: x: 2, y: 2, z: 4, core: 2. Of those that a mesh axis runs over, the one named last changes fastest.
Arguments:
- start_bands: bfloat16 [2048, 1536], P('band', 'elem'), may hold values from -6 to 6
- hamiltonian: bfloat16 [8, 7, 192, 192], P('elem'), may hold values from -0.15625 to 0.15625
- neighbours: int32 [8, 6], P('elem'), may hold values from 0 to 3
- basis_count: int32 [8], P('elem'), may hold values from 128 to 192, as said below
- owner_rows: int32 [16], replicated, may hold values from 1 to 144, 768 in all
- rotation: bfloat16 [2048, 2048], P(None, 'band'), may hold values from -0.125 to 0.125
Outputs:
- filtered: bfloat16 [2048, 1536], P('band', 'elem')
- rotated: bfloat16 [4608, 2048], P(('elem', 'band'))
Inputs may be any that keep to these rules, and one draw needn't show every extreme that they name: `basis_count`: each element holds 128 to 192 basis functions; some element holds exactly 192 and some exactly 128. `neighbours`: any position 0 to 3 may appear in any slot, the element's own position too. `owner_rows`: the entries sum to 768; the largest is exactly 144.
All inputs are finite; a program needn't handle non-finite values.
Results may differ from a plain program's by a relative error of at most 0.013.
Values may be sent and summed in bfloat16 or wider, within the bound.
A program may use at most 64 MiB of HBM per device.

v0:
```python
import functools

import jax
import jax.numpy as jnp
from jax import lax
from jax.experimental import pallas as pl
from jax.experimental.pallas import tpu as pltpu
from jax.sharding import PartitionSpec as P

DEGREE = 8


def padded_2(block, sides, width):
    for axis, dim in sides:
        count = lax.axis_size(axis)
        forward = [(i, i + 1) for i in range(count - 1)]
        forward.append((count - 1, 0))
        backward = [(target, source) for source, target in forward]
        low = lax.ppermute(
            lax.slice_in_dim(block, block.shape[dim] - width, None, axis=dim), axis, forward
        )
        high = lax.ppermute(lax.slice_in_dim(block, 0, width, axis=dim), axis, backward)
        block = jnp.concatenate([low, block, high], axis=dim)
    return block


def per_device(start_bands, hamiltonian, neighbours, basis_count, owner_rows, rotation):
    bands_dev, rows_dev = start_bands.shape
    elem_count = hamiltonian.shape[0]
    basis_max = hamiltonian.shape[2]
    planes_dev = elem_count // 4
    basis_ids = lax.broadcasted_iota(jnp.int32, (elem_count, basis_max), 1)
    row_mask = (basis_ids < basis_count[:, None]).astype(jnp.float32).reshape(rows_dev)
    partner_pick = (neighbours[:, :, None] == jnp.arange(4, dtype=jnp.int32)[None, None, :]).astype(
        jnp.bfloat16
    )
    partner_pick = partner_pick.reshape(planes_dev, 4, 6, 4)
    weights = hamiltonian.reshape(elem_count, 7 * basis_max, basis_max)

    def apply_ham(state):
        plane_slab = state.reshape(bands_dev, planes_dev, 4 * basis_max)
        extended = padded_2(plane_slab, (("elem", 1),), 1)
        extended = extended.reshape(bands_dev, planes_dev + 2, 4, basis_max)
        plane_below = extended[:, :planes_dev]
        plane_mid = extended[:, 1 : planes_dev + 1]
        plane_above = extended[:, 2:]
        inplane = jnp.einsum(
            "pism,bpmk->bpisk",
            partner_pick[:, :, :4],
            plane_mid,
            preferred_element_type=jnp.float32,
        ).astype(jnp.bfloat16)
        lower = jnp.einsum(
            "pim,bpmk->bpik", partner_pick[:, :, 4], plane_below, preferred_element_type=jnp.float32
        ).astype(jnp.bfloat16)
        upper = jnp.einsum(
            "pim,bpmk->bpik", partner_pick[:, :, 5], plane_above, preferred_element_type=jnp.float32
        ).astype(jnp.bfloat16)
        sources = jnp.concatenate(
            [plane_mid[:, :, :, None], inplane, lower[:, :, :, None], upper[:, :, :, None]], axis=3
        )
        sources = sources.reshape(bands_dev, elem_count, 7 * basis_max)
        product = jnp.einsum("bej,ejl->bel", sources, weights, preferred_element_type=jnp.float32)
        return product.reshape(bands_dev, rows_dev) * row_mask

    earlier = (start_bands.astype(jnp.float32) * row_mask).astype(jnp.bfloat16)
    current = (0.5 * apply_ham(earlier)).astype(jnp.bfloat16)
    for repeat in range(DEGREE - 1):
        following = (apply_ham(current) - earlier.astype(jnp.float32)).astype(jnp.bfloat16)
        earlier = current
        current = following
    owners = lax.axis_size("band")
    slot_cap = 3 * rows_dev // owners
    before = jnp.arange(owners)[None, :] < jnp.arange(owners)[:, None]
    row_starts = jnp.sum(jnp.where(before, owner_rows[None, :], 0), axis=1)
    slot_keep = jnp.arange(slot_cap, dtype=jnp.int32)[None, :] < owner_rows[:, None]
    padded = jnp.concatenate([current, jnp.zeros((bands_dev, slot_cap), jnp.bfloat16)], axis=1)
    pieces = jax.vmap(lambda offset: lax.dynamic_slice_in_dim(padded, offset, slot_cap, 1))(
        row_starts
    )
    owned_rows = lax.all_to_all(
        jnp.where(slot_keep[:, None, :], pieces, jnp.zeros((), jnp.bfloat16)),
        "band",
        split_axis=0,
        concat_axis=1,
        tiled=True,
    ).reshape(-1, slot_cap)
    rotated = lax.dot_general(
        owned_rows,
        lax.all_gather(rotation, "band", axis=1, tiled=True),
        (((0,), (0,)), ((), ())),
        preferred_element_type=jnp.float32,
    ).astype(jnp.bfloat16)
    return (current, rotated)


def filter_kernel(
    owners,
    start_ref,
    ham_ref,
    nb_ref,
    count_ref,
    owner_ref,
    filtered_ref,
    owned_ref,
    amat,
    bands,
    masked,
    swapped,
    pieces,
    arrived,
    band_send,
    band_recv,
    strip_send,
    strip_recv,
    core_send,
    core_recv,
    back_send,
    back_recv,
    piece_send,
    piece_recv,
):
    e = lax.axis_index("elem")
    b = lax.axis_index("band")
    o = 1 - e
    core = lax.rem(b, 2)
    sib = b + 1 - 2 * core
    count, rows = start_ref.shape
    half = count // 2
    nb = ham_ref.shape[2]
    cap = owned_ref.shape[0]

    barrier = pltpu.get_barrier_semaphore()
    pl.semaphore_signal(barrier, inc=1, device_id={"elem": o}, device_id_type=pl.DeviceIdType.MESH)

    def greet(d, carry):
        j = lax.rem(b + d, owners)
        pl.semaphore_signal(
            barrier, inc=1, device_id={"band": j}, device_id_type=pl.DeviceIdType.MESH
        )
        return carry

    lax.fori_loop(1, owners, greet, 0)
    pl.semaphore_wait(barrier, owners)

    lane = lax.broadcasted_iota(jnp.int32, (1, rows), 1)
    keep = jnp.zeros((1, rows), jnp.float32)
    for i in range(4):
        inside = (lane >= nb * i) & (lane < nb * i + count_ref[i])
        keep = jnp.where(inside, 1.0, keep)
    masked[...] = (start_ref[...].astype(jnp.float32) * keep).astype(jnp.bfloat16)
    own_cols = pl.ds(pl.multiple_of(rows * e, 128), rows)
    other_cols = pl.ds(pl.multiple_of(rows * o, 128), rows)
    own_half = pl.ds(pl.multiple_of(half * e, 16), half)
    other_half = pl.ds(pl.multiple_of(half * o, 16), half)
    band_copy = pltpu.make_async_remote_copy(
        src_ref=masked.at[other_half],
        dst_ref=bands.at[0, :, own_cols],
        send_sem=band_send,
        recv_sem=band_recv,
        device_id={"elem": o},
        device_id_type=pl.DeviceIdType.MESH,
    )
    band_copy.start()
    bands[0, :, own_cols] = masked[own_half, :]

    def strip_rows(step, side):
        t = 4 * side + step
        return pl.ds(pl.multiple_of(t * nb, 16), nb)

    def build(step, side):
        t = 4 * side + step
        parts = []
        for i in range(4):
            total = jnp.where(t == 4 * e + i, 1.0, 0.0) * ham_ref[i, 0].astype(jnp.float32)
            for j in range(1, 7):
                plane = e if j < 5 else o
                pick = jnp.where(nb_ref[i, j - 1] + 4 * plane == t, 1.0, 0.0)
                total = total + pick * ham_ref[i, j].astype(jnp.float32)
            parts.append(total)
        strip = jnp.concatenate(parts, axis=1) * keep
        amat[e, strip_rows(step, side), :] = strip.astype(jnp.bfloat16)

    def to_partner(step):
        where = strip_rows(step, core)
        return pltpu.make_async_remote_copy(
            src_ref=amat.at[e, where],
            dst_ref=amat.at[e, where],
            send_sem=strip_send.at[step],
            recv_sem=strip_recv.at[step],
            device_id={"elem": o},
            device_id_type=pl.DeviceIdType.MESH,
        )

    def from_partner(step):
        where = strip_rows(step, core)
        return pltpu.make_async_remote_copy(
            src_ref=amat.at[o, where],
            dst_ref=amat.at[o, where],
            send_sem=strip_send.at[step],
            recv_sem=strip_recv.at[step],
            device_id={"elem": o},
            device_id_type=pl.DeviceIdType.MESH,
        )

    def to_sibling(step, side):
        where = strip_rows(step, side)
        return pltpu.make_async_remote_copy(
            src_ref=amat.at[o, where],
            dst_ref=amat.at[o, where],
            send_sem=core_send.at[step],
            recv_sem=core_recv.at[step],
            device_id={"band": sib},
            device_id_type=pl.DeviceIdType.MESH,
        )

    def first_half(step, carry):
        build(step, core)
        to_partner(step).start()
        return carry

    def second_half(step, carry):
        build(step, 1 - core)
        return carry

    def forward(step, carry):
        from_partner(step).wait_recv()
        to_sibling(step, core).start()
        return carry

    def collect(step, carry):
        to_sibling(step, 1 - core).wait_recv()
        to_sibling(step, core).wait_send()
        to_partner(step).wait_send()
        return carry

    lax.fori_loop(0, 4, first_half, 0)
    lax.fori_loop(0, 4, second_half, 0)
    lax.fori_loop(0, 4, forward, 0)
    lax.fori_loop(0, 4, collect, 0)
    band_copy.wait_send()
    pltpu.make_async_remote_copy(
        src_ref=masked.at[other_half],
        dst_ref=bands.at[0, :, other_cols],
        send_sem=band_send,
        recv_sem=band_recv,
        device_id={"elem": o},
        device_id_type=pl.DeviceIdType.MESH,
    ).wait_recv()

    wide = 256 if rows % 256 == 0 else rows

    def advance(now, later, first):
        for p in range(2):
            for c in range(rows // wide):
                product = jnp.dot(
                    bands[now],
                    amat[p, :, c * wide : (c + 1) * wide],
                    preferred_element_type=jnp.float32,
                )
                cols = slice(p * rows + c * wide, p * rows + (c + 1) * wide)
                if first:
                    product = 0.5 * product
                else:
                    product = product - bands[later, :, cols].astype(jnp.float32)
                bands[later, :, cols] = product.astype(jnp.bfloat16)

    advance(0, 1, True)

    def two_steps(k, carry):
        advance(1, 0, False)
        advance(0, 1, False)
        return carry

    lax.fori_loop(0, (DEGREE - 2) // 2, two_steps, 0)
    advance(1, 0, False)

    back = pltpu.make_async_remote_copy(
        src_ref=bands.at[0, :, other_cols],
        dst_ref=swapped,
        send_sem=back_send,
        recv_sem=back_recv,
        device_id={"elem": o},
        device_id_type=pl.DeviceIdType.MESH,
    )
    back.start()
    masked[own_half, :] = bands[0, :, own_cols]
    back.wait()
    masked[other_half, :] = swapped[...]
    filtered_ref[...] = masked[...]

    lanes = lax.broadcasted_iota(jnp.int32, (cap, rows), 1)
    slots = lax.broadcasted_iota(jnp.int32, (cap, rows), 0)

    def piece(j):
        begin = jnp.int32(0)
        for i in range(owners):
            begin = begin + jnp.where(i < j, owner_ref[i], 0)
        chosen = (lanes == slots + begin) & (slots < owner_ref[j])
        pick = jnp.where(chosen, 1.0, 0.0).astype(jnp.bfloat16)
        return lax.dot_general(
            pick, masked[...], (((1,), (1,)), ((), ())), preferred_element_type=jnp.float32
        ).astype(jnp.bfloat16)

    def piece_copy(j, origin):
        return pltpu.make_async_remote_copy(
            src_ref=pieces.at[j],
            dst_ref=arrived.at[origin],
            send_sem=piece_send.at[j],
            recv_sem=piece_recv.at[origin],
            device_id={"band": j},
            device_id_type=pl.DeviceIdType.MESH,
        )

    def send(d, carry):
        j = lax.rem(b + d, owners)
        pieces[j] = piece(j)
        piece_copy(j, b).start()
        return carry

    lax.fori_loop(1, owners, send, 0)
    arrived[b] = piece(b)

    def receive(d, carry):
        j = lax.rem(b + d, owners)
        piece_copy(j, j).wait_recv()
        piece_copy(j, b).wait_send()
        return carry

    lax.fori_loop(1, owners, receive, 0)
    for i in range(owners):
        owned_ref[:, i * count : (i + 1) * count] = arrived[i]


def turn_kernel(owned_ref, rotation_ref, out_ref):
    wide = jnp.concatenate([rotation_ref[0], rotation_ref[1]], axis=1)
    out_ref[...] = jnp.dot(
        owned_ref[...], wide, preferred_element_type=jnp.float32
    ).astype(jnp.bfloat16)


def per_device_pair(start_bands, hamiltonian, neighbours, basis_count, owner_rows, rotation):
    bands_dev, rows_dev = start_bands.shape
    owners = lax.axis_size("band")
    cap = 3 * rows_dev // owners
    bands_all, width = rotation.shape
    nb = hamiltonian.shape[2]
    gathered = lax.all_gather(rotation, "band", axis=0, tiled=False)
    vmem = pl.BlockSpec(memory_space=pltpu.VMEM)
    smem = pl.BlockSpec(memory_space=pltpu.SMEM)
    dma = pltpu.SemaphoreType.DMA
    bf16 = jnp.bfloat16
    filtered, owned = pl.pallas_call(
        functools.partial(filter_kernel, owners),
        out_shape=(
            jax.ShapeDtypeStruct((bands_dev, rows_dev), bf16),
            jax.ShapeDtypeStruct((cap, bands_all), bf16),
        ),
        in_specs=[vmem, vmem, smem, smem, smem],
        out_specs=(vmem, vmem),
        scratch_shapes=[
            pltpu.VMEM((2, 2 * rows_dev, rows_dev), bf16),
            pltpu.VMEM((2, bands_dev // 2, 2 * rows_dev), bf16),
            pltpu.VMEM((bands_dev, rows_dev), bf16),
            pltpu.VMEM((bands_dev // 2, rows_dev), bf16),
            pltpu.VMEM((owners, cap, bands_dev), bf16),
            pltpu.VMEM((owners, cap, bands_dev), bf16),
            dma,
            dma,
            dma((4,)),
            dma((4,)),
            dma((4,)),
            dma((4,)),
            dma,
            dma,
            dma((owners,)),
            dma((owners,)),
        ],
        compiler_params=pltpu.CompilerParams(
            collective_id=0, has_side_effects=True, vmem_limit_bytes=40 * 1024 * 1024
        ),
        cost_estimate=pl.CostEstimate(
            flops=16 * bands_dev * 2 * rows_dev * rows_dev,
            bytes_accessed=200_000_000,
            transcendentals=0,
        ),
    )(start_bands, hamiltonian, neighbours, basis_count, owner_rows)
    rotated = pl.pallas_call(
        turn_kernel,
        grid=(owners // 2,),
        out_shape=jax.ShapeDtypeStruct((cap, owners * width), bf16),
        in_specs=[
            pl.BlockSpec((cap, bands_all), lambda s: (0, 0)),
            pl.BlockSpec((2, bands_all, width), lambda s: (s, 0, 0)),
        ],
        out_specs=pl.BlockSpec((cap, 2 * width), lambda s: (0, s)),
        compiler_params=pltpu.CompilerParams(vmem_limit_bytes=24 * 1024 * 1024),
    )(owned, gathered)
    return filtered, rotated


def solution(mesh):
    pair = mesh.shape["elem"] == 2 and mesh.shape["band"] % 2 == 0
    placed = (
        P("band", "elem"),
        P("elem", None, None, None),
        P("elem", None),
        P("elem"),
        P(),
        P(None, "band"),
    )
    return jax.shard_map(
        per_device_pair if pair else per_device,
        mesh=mesh,
        in_specs=placed,
        out_specs=(P("band", "elem"), P(("elem", "band"), None)),
        check_vma=False,
    )
```

profile of v0, /device:TPU:0, one launch (start us, length us, event | category | flops | bytes accessed | tf_op | source)
XLA Modules:
  0.0 113.1 jit_solution(18324113016030701391)
XLA Ops:
  7.2 0.0 all-gather.3.cloned.1.call-start
  7.2 0.7 all-gather.3.cloned.1.call-update
  7.9 0.0 copy-start.1
  7.9 1.8 %copy-done.1 = bf16[4,7,192,192]{3,2,1,0:T(8,128)(2,1)S(1)} copy-done((bf16[4,7,192,192]{3,2,1,0:T(8,128)(2,1)S(1)}, bf16[4,7,192,192]{3,2,1,0:T(8,128)(2,1)}, u32[]{:S(2)}) %copy-start.1) | copy-done | bytes 2064408
  9.7 0.0 copy-start.2
  9.7 0.9 copy-done.2
  10.6 0.0 copy-start.3
  10.6 0.7 copy-done.3
  11.3 0.0 copy-start.4
  11.3 0.7 copy-done.4
  11.9 0.0 copy-start.5
  11.9 0.7 copy-done.5
  12.6 67.2 %shard_map.77 = (bf16[128,768]{1,0:T(8,128)(2,1)S(1)}, bf16[144,2048]{1,0:T(8,128)(2,1)S(1)}) custom-call(bf16[128,768]{1,0:T(8,128)(2,1)S(1)} %copy-done.2, bf16[4,7,192,192]{3,2,1,0:T(8,128)(2,1)S(1)} %copy-done.1, s32[4,6]{1,0:T(4,128)S(1)} %copy-done.3, s32[4]{0:T(128)S(1)} %copy-done.4, s32[16]{0:T(128)S(1)} %copy-done.5), custom_call_target="tpu_custom_call" | custom-call | flops 2415919104 | bytes 200000000 | tf_op jit(solution)/shard_map/pallas_call | solution.py:353
  79.8 18.2 %all-gather.3.cloned.1.call-done = bf16[32768,128]{1,0:T(8,128)(2,1)} async-done(((bf16[2048,128]{1,0:T(8,128)(2,1)}), bf16[32768,128]{1,0:T(8,128)(2,1)}) %all-gather.3.cloned.1.call-update) | async-done | bytes 8388624 | tf_op jit(solution)/shard_map/all_gather | solution.py:348
  98.0 0.0 copy-start
  98.0 3.4 %copy-done = bf16[32768,128]{1,0:T(8,128)(2,1)S(1)} copy-done((bf16[32768,128]{1,0:T(8,128)(2,1)S(1)}, bf16[32768,128]{1,0:T(8,128)(2,1)}, u32[]{:S(2)}) %copy-start) | copy-done | bytes 8388632
  101.4 4.2 %shard_map.78 = bf16[144,2048]{1,0:T(8,128)(2,1)} custom-call(bf16[144,2048]{1,0:T(8,128)(2,1)S(1)} %get-tuple-element.5.owned_ref, bf16[16,2048,128]{2,1,0:T(8,128)(2,1)S(1)} %bitcast.1), custom_call_target="tpu_custom_call" | custom-call | tf_op jit(solution)/shard_map/pallas_call | solution.py:388
  105.6 0.7 copy.9
Async XLA Ops:
  7.2 90.8 %all-gather.3.cloned.1.call-start = ((), (), s32[]{:S(2)}) async-start(), calls=%async_computation | async-start | bytes 8912896 | tf_op jit(solution)/shard_map/all_gather | solution.py:348
  7.9 1.8 %copy-start.1 = (bf16[4,7,192,192]{3,2,1,0:T(8,128)(2,1)S(1)}, bf16[4,7,192,192]{3,2,1,0:T(8,128)(2,1)}, u32[]{:S(2)}) copy-start(bf16[4,7,192,192]{3,2,1,0:T(8,128)(2,1)} %ham_ref.1) | copy-start | bytes 6193156
  9.7 0.9 copy-start.2
  10.6 0.7 copy-start.3
  11.3 0.7 copy-start.4
  11.9 0.7 copy-start.5
  98.0 3.4 %copy-start = (bf16[32768,128]{1,0:T(8,128)(2,1)S(1)}, bf16[32768,128]{1,0:T(8,128)(2,1)}, u32[]{:S(2)}) copy-start(bf16[32768,128]{1,0:T(8,128)(2,1)} %all-gather.3.cloned.1.call-done) | copy-start | bytes 25165828
Sparse Core Ops, SparseCore 0:
  10.2 87.7 all-gather.2
where the time goes:
time: 113 us
  Pallas kernels  71.4 us (63%)
  waiting for transfers between devices  18.9 us (17%)
  between operations  14 us (12%)
  local copies, waits for them, and re-layouts  8.74 us (8%)
    pallas_call x1, Pallas kernels, per_device_pair(): pl.pallas_call(functools.partial(filter_kernel, owners), out_shape=(jax.S...  67.2 us
    all_gather x1, waiting for transfers between devices, per_device_pair(): gathered = lax.all_gather(rotation, 'band', axis=0, tiled=False)  18.2 us
    unnamed x13, local copies, waits for them, and re-layouts  8.74 us
    pallas_call x1, Pallas kernels, per_device_pair(): pl.pallas_call(turn_kernel, grid=(owners // 2,), out_shape=jax.ShapeDtype...  4.2 us
  transfers between devices with their start and end apart: 1, of which 1 were waited for; matrix products, arithmetic and copies ran while one was open for 0% of the time, Pallas kernels for 59%

commit v1 on v0

--- a/solution.py
+++ b/solution.py
@@ -101,8 +101,11 @@
     nb_ref,
     count_ref,
     owner_ref,
+    rotation_ref,
     filtered_ref,
+    rotated_ref,
     owned_ref,
+    columns,
     amat,
     bands,
     masked,
@@ -119,6 +122,12 @@
     back_recv,
     piece_send,
     piece_recv,
+    ring_send,
+    ring_recv,
+    share_send,
+    share_recv,
+    mine_send,
+    mine_recv,
 ):
     e = lax.axis_index("elem")
     b = lax.axis_index("band")
@@ -142,6 +151,69 @@
 
     lax.fori_loop(1, owners, greet, 0)
     pl.semaphore_wait(barrier, owners)
+
+    chips = owners // 2
+    tall = chips // 2
+    chip = b // 2
+    layer = chip // 2
+    place = jnp.where(lax.rem(chip, 2) == 0, layer, chips - 1 - layer)
+    depth = rotation_ref.shape[0] // 2
+
+    def member(position, which):
+        position = lax.rem(position + 2 * chips, chips)
+        near = 4 * position
+        far = 4 * (chips - 1 - position) + 2
+        return jnp.where(position < tall, near, far) + which
+
+    def part(chunk, way):
+        return columns.at[chunk, pl.ds(way * depth, depth)]
+
+    def ring_copy(step, way, chunk):
+        return pltpu.make_async_remote_copy(
+            src_ref=part(chunk, way),
+            dst_ref=part(chunk, way),
+            send_sem=ring_send.at[way, step],
+            recv_sem=ring_recv.at[way, step],
+            device_id={"band": member(place + 1 - 2 * way, core)},
+            device_id_type=pl.DeviceIdType.MESH,
+        )
+
+    def sent_chunk(step, way, which):
+        return member(place - step + 2 * step * way, which)
+
+    def share_copy(step, way, which):
+        chunk = sent_chunk(step + 1, way, which)
+        return pltpu.make_async_remote_copy(
+            src_ref=part(chunk, way),
+            dst_ref=part(chunk, way),
+            send_sem=share_send.at[way, step],
+            recv_sem=share_recv.at[way, step],
+            device_id={"band": sib},
+            device_id_type=pl.DeviceIdType.MESH,
+        )
+
+    def mine_copy(chunk):
+        return pltpu.make_async_remote_copy(
+            src_ref=columns.at[chunk],
+            dst_ref=columns.at[chunk],
+            send_sem=mine_send,
+            recv_sem=mine_recv,
+            device_id={"band": sib},
+            device_id_type=pl.DeviceIdType.MESH,
+        )
+
+    def ring(step):
+        for way in range(2):
+            if step > 0:
+                ring_copy(step - 1, way, sent_chunk(step, way, core)).wait_recv()
+            if step < chips - 1:
+                ring_copy(step, way, sent_chunk(step, way, core)).start()
+            if step > 0:
+                share_copy(step - 1, way, core).start()
+
+    columns[b] = rotation_ref[...]
+    ring(0)
+    mine_copy(b).start()
 
     lane = lax.broadcasted_iota(jnp.int32, (1, rows), 1)
     keep = jnp.zeros((1, rows), jnp.float32)
@@ -236,7 +308,13 @@
 
     lax.fori_loop(0, 4, first_half, 0)
     lax.fori_loop(0, 4, second_half, 0)
-    lax.fori_loop(0, 4, forward, 0)
+    early = max(chips - 3, 0)
+    for step in range(4):
+        if step + 1 <= early:
+            ring(step + 1)
+        forward(step, 0)
+    for step in range(5, early + 1):
+        ring(step)
     lax.fori_loop(0, 4, collect, 0)
     band_copy.wait_send()
     pltpu.make_async_remote_copy(
@@ -284,6 +362,8 @@
         device_id_type=pl.DeviceIdType.MESH,
     )
     back.start()
+    for step in range(early + 1, chips - 1):
+        ring(step)
     masked[own_half, :] = bands[0, :, own_cols]
     back.wait()
     masked[other_half, :] = swapped[...]
@@ -327,16 +407,28 @@
         piece_copy(j, b).wait_send()
         return carry
 
+    ring(chips - 1)
     lax.fori_loop(1, owners, receive, 0)
     for i in range(owners):
         owned_ref[:, i * count : (i + 1) * count] = arrived[i]
-
-
-def turn_kernel(owned_ref, rotation_ref, out_ref):
-    wide = jnp.concatenate([rotation_ref[0], rotation_ref[1]], axis=1)
-    out_ref[...] = jnp.dot(
-        owned_ref[...], wide, preferred_element_type=jnp.float32
-    ).astype(jnp.bfloat16)
+    mine_copy(b).wait_send()
+    mine_copy(sib).wait_recv()
+    for step in range(chips - 1):
+        for way in range(2):
+            ring_copy(step, way, sent_chunk(step, way, core)).wait_send()
+            share_copy(step, way, core).wait_send()
+            share_copy(step, way, 1 - core).wait_recv()
+    width = rotation_ref.shape[1]
+
+    def turn(pair, carry):
+        wide = jnp.concatenate([columns[2 * pair], columns[2 * pair + 1]], axis=1)
+        where = pl.ds(pl.multiple_of(pair * 2 * width, 128), 2 * width)
+        rotated_ref[:, where] = jnp.dot(
+            owned_ref[...], wide, preferred_element_type=jnp.float32
+        ).astype(jnp.bfloat16)
+        return carry
+
+    lax.fori_loop(0, owners // 2, turn, 0)
 
 
 def per_device_pair(start_bands, hamiltonian, neighbours, basis_count, owner_rows, rotation):
@@ -344,21 +436,22 @@
     owners = lax.axis_size("band")
     cap = 3 * rows_dev // owners
     bands_all, width = rotation.shape
-    nb = hamiltonian.shape[2]
-    gathered = lax.all_gather(rotation, "band", axis=0, tiled=False)
+    hops = owners // 2 - 1
     vmem = pl.BlockSpec(memory_space=pltpu.VMEM)
     smem = pl.BlockSpec(memory_space=pltpu.SMEM)
     dma = pltpu.SemaphoreType.DMA
     bf16 = jnp.bfloat16
-    filtered, owned = pl.pallas_call(
+    return pl.pallas_call(
         functools.partial(filter_kernel, owners),
         out_shape=(
             jax.ShapeDtypeStruct((bands_dev, rows_dev), bf16),
-            jax.ShapeDtypeStruct((cap, bands_all), bf16),
+            jax.ShapeDtypeStruct((cap, owners * width), bf16),
         ),
-        in_specs=[vmem, vmem, smem, smem, smem],
+        in_specs=[vmem, vmem, smem, smem, smem, vmem],
         out_specs=(vmem, vmem),
         scratch_shapes=[
+            pltpu.VMEM((cap, bands_all), bf16),
+            pltpu.VMEM((owners, bands_all, width), bf16),
             pltpu.VMEM((2, 2 * rows_dev, rows_dev), bf16),
             pltpu.VMEM((2, bands_dev // 2, 2 * rows_dev), bf16),
             pltpu.VMEM((bands_dev, rows_dev), bf16),
@@ -375,6 +468,12 @@
             dma,
             dma((owners,)),
             dma((owners,)),
+            dma((2, hops)),
+            dma((2, hops)),
+            dma((2, hops)),
+            dma((2, hops)),
+            dma,
+            dma,
         ],
         compiler_params=pltpu.CompilerParams(
             collective_id=0, has_side_effects=True, vmem_limit_bytes=40 * 1024 * 1024
@@ -384,23 +483,11 @@
             bytes_accessed=200_000_000,
             transcendentals=0,
         ),
-    )(start_bands, hamiltonian, neighbours, basis_count, owner_rows)
-    rotated = pl.pallas_call(
-        turn_kernel,
-        grid=(owners // 2,),
-        out_shape=jax.ShapeDtypeStruct((cap, owners * width), bf16),
-        in_specs=[
-            pl.BlockSpec((cap, bands_all), lambda s: (0, 0)),
-            pl.BlockSpec((2, bands_all, width), lambda s: (s, 0, 0)),
-        ],
-        out_specs=pl.BlockSpec((cap, 2 * width), lambda s: (0, s)),
-        compiler_params=pltpu.CompilerParams(vmem_limit_bytes=24 * 1024 * 1024),
-    )(owned, gathered)
-    return filtered, rotated
+    )(start_bands, hamiltonian, neighbours, basis_count, owner_rows, rotation)
 
 
 def solution(mesh):
-    pair = mesh.shape["elem"] == 2 and mesh.shape["band"] % 2 == 0
+    pair = mesh.shape["elem"] == 2 and mesh.shape["band"] % 4 == 0
     placed = (
         P("band", "elem"),
         P("elem", None, None, None),

time: 113 us -> 75.9 us (0.67)
  waiting for transfers between devices: 18.9 us -> 0 us
  between operations: 14 us -> 0.65 us
  Pallas kernels: 71.4 us -> 67.5 us
  local copies, waits for them, and re-layouts: 8.74 us -> 7.22 us
    all_gather x1 -> x0, waiting for transfers between devices: 18.2 us -> none  [per_device_pair(): gathered = lax.all_gather(rotation, 'band', axis=0, tiled=False)]
    pallas_call x1 -> x0, Pallas kernels: 4.2 us -> none  [per_device_pair(): pl.pallas_call(turn_kernel, grid=(owners // 2,), out_shape=jax.ShapeDtype...]
    unnamed x13 -> x14, local copies, waits for them, and re-layouts: 8.74 us -> 7.22 us
  transfers between devices with their start and end apart: 1 -> 0, of which waited for: 1 -> 0; matrix products, arithmetic and copies ran while one was open for 0% -> 0% of each run, Pallas kernels for 59% -> 0%
where the time goes in v1:
time: 75.9 us; the launch traced here: 75.3 us
  Pallas kernels  67.5 us (89%)
  local copies, waits for them, and re-layouts  7.22 us (10%)
    pallas_call x1, Pallas kernels, per_device_pair(): pl.pallas_call(functools.partial(filter_kernel, owners), out_shape=(jax.S...  67.5 us
    unnamed x14, local copies, waits for them, and re-layouts  7.22 us

profile of v1, /device:TPU:0, one launch (start us, length us, event | category | flops | bytes accessed | tf_op | source)
XLA Modules:
  0.0 75.3 jit_solution(4011993345857383481)
XLA Ops:
  0.6 0.0 copy-start
  0.6 1.8 %copy-done = bf16[4,7,192,192]{3,2,1,0:T(8,128)(2,1)S(1)} copy-done((bf16[4,7,192,192]{3,2,1,0:T(8,128)(2,1)S(1)}, bf16[4,7,192,192]{3,2,1,0:T(8,128)(2,1)}, u32[]{:S(2)}) %copy-start) | copy-done | bytes 2064408
  2.4 0.0 copy-start.1
  2.4 1.0 %copy-done.1 = bf16[2048,128]{1,0:T(8,128)(2,1)S(1)} copy-done((bf16[2048,128]{1,0:T(8,128)(2,1)S(1)}, bf16[2048,128]{1,0:T(8,128)(2,1)}, u32[]{:S(2)}) %copy-start.1) | copy-done | bytes 524312
  3.5 0.0 copy-start.2
  3.5 0.9 %copy-done.2 = bf16[128,768]{1,0:T(8,128)(2,1)S(1)} copy-done((bf16[128,768]{1,0:T(8,128)(2,1)S(1)}, bf16[128,768]{1,0:T(8,128)(2,1)}, u32[]{:S(2)}) %copy-start.2) | copy-done | bytes 196632
  4.4 0.0 copy-start.3
  4.4 0.7 copy-done.3
  5.1 0.0 copy-start.4
  5.1 0.7 copy-done.4
  5.7 0.0 copy-start.5
  5.7 0.7 copy-done.5
  6.4 67.5 %shard_map.77 = (bf16[128,768]{1,0:T(8,128)(2,1)S(1)}, bf16[144,2048]{1,0:T(8,128)(2,1)S(1)}) custom-call(bf16[128,768]{1,0:T(8,128)(2,1)S(1)} %copy-done.2, bf16[4,7,192,192]{3,2,1,0:T(8,128)(2,1)S(1)} %copy-done, s32[4,6]{1,0:T(4,128)S(1)} %copy-done.3, s32[4]{0:T(128)S(1)} %copy-done.4, s32[16]{0:T(128)S(1)} %copy-done.5, bf16[2048,128]{1,0:T(8,128)(2,1)S(1)} %copy-done.1), custom_call_target="tpu_custom_call" | custom-call | flops 2415919104 | bytes 200000000 | tf_op jit(solution)/shard_map/pallas_call | solution.py:444
  73.9 0.7 copy.10
  74.5 0.8 %copy.11 = bf16[144,2048]{1,0:T(8,128)(2,1)} copy(bf16[144,2048]{1,0:T(8,128)(2,1)S(1)} %get-tuple-element.5) | data formatting | bytes 1179648
Async XLA Ops:
  0.6 1.8 %copy-start = (bf16[4,7,192,192]{3,2,1,0:T(8,128)(2,1)S(1)}, bf16[4,7,192,192]{3,2,1,0:T(8,128)(2,1)}, u32[]{:S(2)}) copy-start(bf16[4,7,192,192]{3,2,1,0:T(8,128)(2,1)} %ham_ref.1) | copy-start | bytes 6193156
  2.4 1.0 %copy-start.1 = (bf16[2048,128]{1,0:T(8,128)(2,1)S(1)}, bf16[2048,128]{1,0:T(8,128)(2,1)}, u32[]{:S(2)}) copy-start(bf16[2048,128]{1,0:T(8,128)(2,1)} %rotation_ref.1) | copy-start | bytes 1572868
  3.5 0.9 %copy-start.2 = (bf16[128,768]{1,0:T(8,128)(2,1)S(1)}, bf16[128,768]{1,0:T(8,128)(2,1)}, u32[]{:S(2)}) copy-start(bf16[128,768]{1,0:T(8,128)(2,1)} %start_ref.1) | copy-start | bytes 589828
  4.4 0.7 copy-start.3
  5.1 0.7 copy-start.4
  5.7 0.7 copy-start.5

commit v2 on v1

--- a/solution.py
+++ b/solution.py
@@ -96,12 +96,12 @@
 
 def filter_kernel(
     owners,
-    start_ref,
-    ham_ref,
+    start_hbm,
+    ham_hbm,
     nb_ref,
     count_ref,
     owner_ref,
-    rotation_ref,
+    rotation_hbm,
     filtered_ref,
     rotated_ref,
     owned_ref,
@@ -128,12 +128,25 @@
     share_recv,
     mine_send,
     mine_recv,
+    start_ref,
+    ham_ref,
+    load_sem,
+    side_send,
+    side_recv,
+    second_send,
+    second_recv,
 ):
     e = lax.axis_index("elem")
     b = lax.axis_index("band")
     o = 1 - e
     core = lax.rem(b, 2)
     sib = b + 1 - 2 * core
+    load_rotation = pltpu.make_async_copy(rotation_hbm, columns.at[b], load_sem.at[0])
+    load_start = pltpu.make_async_copy(start_hbm, start_ref, load_sem.at[1])
+    load_ham = pltpu.make_async_copy(ham_hbm, ham_ref, load_sem.at[2])
+    load_rotation.start()
+    load_start.start()
+    load_ham.start()
     count, rows = start_ref.shape
     half = count // 2
     nb = ham_ref.shape[2]
@@ -157,7 +170,7 @@
     chip = b // 2
     layer = chip // 2
     place = jnp.where(lax.rem(chip, 2) == 0, layer, chips - 1 - layer)
-    depth = rotation_ref.shape[0] // 2
+    depth = rotation_hbm.shape[0] // 2
 
     def member(position, which):
         position = lax.rem(position + 2 * chips, chips)
@@ -211,9 +224,17 @@
             if step > 0:
                 share_copy(step - 1, way, core).start()
 
-    columns[b] = rotation_ref[...]
+    passed = [0]
+
+    def ring_next():
+        if passed[0] < chips - 1:
+            passed[0] += 1
+            ring(passed[0])
+
+    load_rotation.wait()
     ring(0)
     mine_copy(b).start()
+    load_start.wait()
 
     lane = lax.broadcasted_iota(jnp.int32, (1, rows), 1)
     keep = jnp.zeros((1, rows), jnp.float32)
@@ -236,12 +257,19 @@
     band_copy.start()
     bands[0, :, own_cols] = masked[own_half, :]
 
-    def strip_rows(step, side):
-        t = 4 * side + step
+    thin = nb // 2
+    beside = lax.rem(chip, 2)
+    quarter = 2 * beside + core
+    beside_quarter = 2 * (1 - beside) + core
+    across = b + 2 - 4 * beside
+
+    def strip_rows(t):
         return pl.ds(pl.multiple_of(t * nb, 16), nb)
 
-    def build(step, side):
-        t = 4 * side + step
+    def thin_rows(step, which):
+        return pl.ds(pl.multiple_of(2 * nb * which + step * thin, 16), thin)
+
+    def build(t):
         parts = []
         for i in range(4):
             total = jnp.where(t == 4 * e + i, 1.0, 0.0) * ham_ref[i, 0].astype(jnp.float32)
@@ -251,70 +279,75 @@
                 total = total + pick * ham_ref[i, j].astype(jnp.float32)
             parts.append(total)
         strip = jnp.concatenate(parts, axis=1) * keep
-        amat[e, strip_rows(step, side), :] = strip.astype(jnp.bfloat16)
+        amat[e, strip_rows(t), :] = strip.astype(jnp.bfloat16)
+
+    def move(plane, step, which, send, recv, device):
+        where = thin_rows(step, which)
+        return pltpu.make_async_remote_copy(
+            src_ref=amat.at[plane, where],
+            dst_ref=amat.at[plane, where],
+            send_sem=send.at[step],
+            recv_sem=recv.at[step],
+            device_id=device,
+            device_id_type=pl.DeviceIdType.MESH,
+        )
 
     def to_partner(step):
-        where = strip_rows(step, core)
-        return pltpu.make_async_remote_copy(
-            src_ref=amat.at[e, where],
-            dst_ref=amat.at[e, where],
-            send_sem=strip_send.at[step],
-            recv_sem=strip_recv.at[step],
-            device_id={"elem": o},
-            device_id_type=pl.DeviceIdType.MESH,
-        )
+        return move(e, step, quarter, strip_send, strip_recv, {"elem": o})
 
     def from_partner(step):
-        where = strip_rows(step, core)
-        return pltpu.make_async_remote_copy(
-            src_ref=amat.at[o, where],
-            dst_ref=amat.at[o, where],
-            send_sem=strip_send.at[step],
-            recv_sem=strip_recv.at[step],
-            device_id={"elem": o},
-            device_id_type=pl.DeviceIdType.MESH,
-        )
-
-    def to_sibling(step, side):
-        where = strip_rows(step, side)
-        return pltpu.make_async_remote_copy(
-            src_ref=amat.at[o, where],
-            dst_ref=amat.at[o, where],
-            send_sem=core_send.at[step],
-            recv_sem=core_recv.at[step],
-            device_id={"band": sib},
-            device_id_type=pl.DeviceIdType.MESH,
-        )
-
-    def first_half(step, carry):
-        build(step, core)
-        to_partner(step).start()
-        return carry
-
-    def second_half(step, carry):
-        build(step, 1 - core)
-        return carry
-
-    def forward(step, carry):
+        return move(o, step, quarter, strip_send, strip_recv, {"elem": o})
+
+    def to_side(step, which):
+        return move(o, step, which, side_send, side_recv, {"band": across})
+
+    def to_sibling(step, which):
+        return move(o, step, which, core_send, core_recv, {"band": sib})
+
+    def second_to_sibling(step, which):
+        return move(o, step, which, second_send, second_recv, {"band": sib})
+
+    def first_build(step, carry):
+        build(2 * quarter + step)
+        for k in range(2):
+            to_partner(2 * step + k).start()
+        return carry
+
+    def other_build(step, carry):
+        build(lax.rem(2 * quarter + step, 8))
+        return carry
+
+    def forward(step):
         from_partner(step).wait_recv()
-        to_sibling(step, core).start()
-        return carry
+        to_side(step, quarter).start()
+        to_sibling(step, quarter).start()
+
+    def second_forward(step):
+        to_side(step, beside_quarter).wait_recv()
+        second_to_sibling(step, beside_quarter).start()
 
     def collect(step, carry):
-        to_sibling(step, 1 - core).wait_recv()
-        to_sibling(step, core).wait_send()
+        to_sibling(step, 2 * beside + 1 - core).wait_recv()
+        second_to_sibling(step, 2 * (1 - beside) + 1 - core).wait_recv()
         to_partner(step).wait_send()
-        return carry
-
-    lax.fori_loop(0, 4, first_half, 0)
-    lax.fori_loop(0, 4, second_half, 0)
-    early = max(chips - 3, 0)
-    for step in range(4):
-        if step + 1 <= early:
-            ring(step + 1)
-        forward(step, 0)
-    for step in range(5, early + 1):
-        ring(step)
+        to_side(step, quarter).wait_send()
+        to_sibling(step, quarter).wait_send()
+        second_to_sibling(step, beside_quarter).wait_send()
+        return carry
+
+    load_ham.wait()
+    lax.fori_loop(0, 2, first_build, 0)
+    lax.fori_loop(2, 8, other_build, 0)
+    forward(0)
+    forward(1)
+    ring_next()
+    forward(2)
+    second_forward(0)
+    forward(3)
+    second_forward(1)
+    ring_next()
+    second_forward(2)
+    second_forward(3)
     lax.fori_loop(0, 4, collect, 0)
     band_copy.wait_send()
     pltpu.make_async_remote_copy(
@@ -350,7 +383,11 @@
         advance(0, 1, False)
         return carry
 
-    lax.fori_loop(0, (DEGREE - 2) // 2, two_steps, 0)
+    split = (DEGREE - 2) // 4
+    lax.fori_loop(0, split, two_steps, 0)
+    ring_next()
+    lax.fori_loop(split, (DEGREE - 2) // 2, two_steps, 0)
+    ring_next()
     advance(1, 0, False)
 
     back = pltpu.make_async_remote_copy(
@@ -362,8 +399,7 @@
         device_id_type=pl.DeviceIdType.MESH,
     )
     back.start()
-    for step in range(early + 1, chips - 1):
-        ring(step)
+    ring_next()
     masked[own_half, :] = bands[0, :, own_cols]
     back.wait()
     masked[other_half, :] = swapped[...]
@@ -398,7 +434,9 @@
         piece_copy(j, b).start()
         return carry
 
-    lax.fori_loop(1, owners, send, 0)
+    lax.fori_loop(1, owners // 2, send, 0)
+    ring_next()
+    lax.fori_loop(owners // 2, owners, send, 0)
     arrived[b] = piece(b)
 
     def receive(d, carry):
@@ -407,7 +445,8 @@
         piece_copy(j, b).wait_send()
         return carry
 
-    ring(chips - 1)
+    while passed[0] < chips - 1:
+        ring_next()
     lax.fori_loop(1, owners, receive, 0)
     for i in range(owners):
         owned_ref[:, i * count : (i + 1) * count] = arrived[i]
@@ -418,7 +457,7 @@
             ring_copy(step, way, sent_chunk(step, way, core)).wait_send()
             share_copy(step, way, core).wait_send()
             share_copy(step, way, 1 - core).wait_recv()
-    width = rotation_ref.shape[1]
+    width = rotation_hbm.shape[1]
 
     def turn(pair, carry):
         wide = jnp.concatenate([columns[2 * pair], columns[2 * pair + 1]], axis=1)
@@ -438,6 +477,7 @@
     bands_all, width = rotation.shape
     hops = owners // 2 - 1
     vmem = pl.BlockSpec(memory_space=pltpu.VMEM)
+    hbm = pl.BlockSpec(memory_space=pltpu.HBM)
     smem = pl.BlockSpec(memory_space=pltpu.SMEM)
     dma = pltpu.SemaphoreType.DMA
     bf16 = jnp.bfloat16
@@ -447,7 +487,7 @@
             jax.ShapeDtypeStruct((bands_dev, rows_dev), bf16),
             jax.ShapeDtypeStruct((cap, owners * width), bf16),
         ),
-        in_specs=[vmem, vmem, smem, smem, smem, vmem],
+        in_specs=[hbm, hbm, smem, smem, smem, hbm],
         out_specs=(vmem, vmem),
         scratch_shapes=[
             pltpu.VMEM((cap, bands_all), bf16),
@@ -474,6 +514,13 @@
             dma((2, hops)),
             dma,
             dma,
+            pltpu.VMEM(start_bands.shape, bf16),
+            pltpu.VMEM(hamiltonian.shape, bf16),
+            dma((3,)),
+            dma((4,)),
+            dma((4,)),
+            dma((4,)),
+            dma((4,)),
         ],
         compiler_params=pltpu.CompilerParams(
             collective_id=0, has_side_effects=True, vmem_limit_bytes=40 * 1024 * 1024

time: 75.9 us -> 89.6 us (1.18)
  the two profiles are of different devices: /device:TPU:0 before, /device:TPU:17 now
where the time goes in v2:
time: 89.6 us; the launch traced here: 89.3 us
  Pallas kernels  81.4 us (91%)
  local copies, waits for them, and re-layouts  7.22 us (8%)
    pallas_call x1, Pallas kernels, per_device_pair(): pl.pallas_call(functools.partial(filter_kernel, owners), out_shape=(jax.S...  81.4 us
    unnamed x14, local copies, waits for them, and re-layouts  7.22 us

profile of v2, /device:TPU:17, one launch (start us, length us, event | category | flops | bytes accessed | tf_op | source)
XLA Modules:
  0.0 89.3 jit_solution(15280519118241457059)
XLA Ops:
  0.6 0.0 copy-start
  0.6 1.8 %copy-done = bf16[4,7,192,192]{3,2,1,0:T(8,128)(2,1)S(1)} copy-done((bf16[4,7,192,192]{3,2,1,0:T(8,128)(2,1)S(1)}, bf16[4,7,192,192]{3,2,1,0:T(8,128)(2,1)}, u32[]{:S(2)}) %copy-start) | copy-done | bytes 2064408
  2.4 0.0 copy-start.1
  2.4 1.0 %copy-done.1 = bf16[2048,128]{1,0:T(8,128)(2,1)S(1)} copy-done((bf16[2048,128]{1,0:T(8,128)(2,1)S(1)}, bf16[2048,128]{1,0:T(8,128)(2,1)}, u32[]{:S(2)}) %copy-start.1) | copy-done | bytes 524312
  3.5 0.0 copy-start.2
  3.5 0.9 %copy-done.2 = bf16[128,768]{1,0:T(8,128)(2,1)S(1)} copy-done((bf16[128,768]{1,0:T(8,128)(2,1)S(1)}, bf16[128,768]{1,0:T(8,128)(2,1)}, u32[]{:S(2)}) %copy-start.2) | copy-done | bytes 196632
  4.4 0.0 copy-start.3
  4.4 0.7 copy-done.3
  5.1 0.0 copy-start.4
  5.1 0.7 copy-done.4
  5.7 0.0 copy-start.5
  5.7 0.7 copy-done.5
  6.4 81.4 %shard_map.77 = (bf16[128,768]{1,0:T(8,128)(2,1)S(1)}, bf16[144,2048]{1,0:T(8,128)(2,1)S(1)}) custom-call(bf16[128,768]{1,0:T(8,128)(2,1)S(1)} %copy-done.2, bf16[4,7,192,192]{3,2,1,0:T(8,128)(2,1)S(1)} %copy-done, s32[4,6]{1,0:T(4,128)S(1)} %copy-done.3, s32[4]{0:T(128)S(1)} %copy-done.4, s32[16]{0:T(128)S(1)} %copy-done.5, bf16[2048,128]{1,0:T(8,128)(2,1)S(1)} %copy-done.1), custom_call_target="tpu_custom_call" | custom-call | flops 2415919104 | bytes 200000000 | tf_op jit(solution)/shard_map/pallas_call | solution.py:484
  87.8 0.7 copy.10
  88.5 0.8 copy.11
Async XLA Ops:
  0.6 1.8 %copy-start = (bf16[4,7,192,192]{3,2,1,0:T(8,128)(2,1)S(1)}, bf16[4,7,192,192]{3,2,1,0:T(8,128)(2,1)}, u32[]{:S(2)}) copy-start(bf16[4,7,192,192]{3,2,1,0:T(8,128)(2,1)} %ham_hbm.1) | copy-start | bytes 6193156
  2.4 1.0 %copy-start.1 = (bf16[2048,128]{1,0:T(8,128)(2,1)S(1)}, bf16[2048,128]{1,0:T(8,128)(2,1)}, u32[]{:S(2)}) copy-start(bf16[2048,128]{1,0:T(8,128)(2,1)} %rotation_hbm.1) | copy-start | bytes 1572868
  3.5 0.9 %copy-start.2 = (bf16[128,768]{1,0:T(8,128)(2,1)S(1)}, bf16[128,768]{1,0:T(8,128)(2,1)}, u32[]{:S(2)}) copy-start(bf16[128,768]{1,0:T(8,128)(2,1)} %start_hbm.1) | copy-start | bytes 589828
  4.4 0.7 copy-start.3
  5.1 0.7 copy-start.4
  5.7 0.7 copy-start.5

commit v3 on v1

--- a/solution.py
+++ b/solution.py
@@ -212,6 +212,13 @@
                 share_copy(step - 1, way, core).start()
 
     columns[b] = rotation_ref[...]
+    passed = [0]
+
+    def ring_next():
+        if passed[0] < chips - 1:
+            passed[0] += 1
+            ring(passed[0])
+
     ring(0)
     mine_copy(b).start()
 
@@ -308,13 +315,9 @@
 
     lax.fori_loop(0, 4, first_half, 0)
     lax.fori_loop(0, 4, second_half, 0)
-    early = max(chips - 3, 0)
     for step in range(4):
-        if step + 1 <= early:
-            ring(step + 1)
         forward(step, 0)
-    for step in range(5, early + 1):
-        ring(step)
+        ring_next()
     lax.fori_loop(0, 4, collect, 0)
     band_copy.wait_send()
     pltpu.make_async_remote_copy(
@@ -350,7 +353,10 @@
         advance(0, 1, False)
         return carry
 
-    lax.fori_loop(0, (DEGREE - 2) // 2, two_steps, 0)
+    split = (DEGREE - 2) // 4
+    lax.fori_loop(0, split, two_steps, 0)
+    ring_next()
+    lax.fori_loop(split, (DEGREE - 2) // 2, two_steps, 0)
     advance(1, 0, False)
 
     back = pltpu.make_async_remote_copy(
@@ -362,8 +368,7 @@
         device_id_type=pl.DeviceIdType.MESH,
     )
     back.start()
-    for step in range(early + 1, chips - 1):
-        ring(step)
+    ring_next()
     masked[own_half, :] = bands[0, :, own_cols]
     back.wait()
     masked[other_half, :] = swapped[...]
@@ -407,7 +412,8 @@
         piece_copy(j, b).wait_send()
         return carry
 
-    ring(chips - 1)
+    while passed[0] < chips - 1:
+        ring_next()
     lax.fori_loop(1, owners, receive, 0)
     for i in range(owners):
         owned_ref[:, i * count : (i + 1) * count] = arrived[i]

time: 75.9 us -> 78 us (1.028)
  Pallas kernels: 67.5 us -> 69.3 us
    pallas_call x1, Pallas kernels: 67.5 us -> 69.3 us  [per_device_pair(): pl.pallas_call(functools.partial(filter_kernel, owners), out_shape=(jax.S...]
where the time goes in v3:
time: 78 us; the launch traced here: 77.2 us
  Pallas kernels  69.3 us (89%)
  local copies, waits for them, and re-layouts  7.22 us (9%)
    pallas_call x1, Pallas kernels, per_device_pair(): pl.pallas_call(functools.partial(filter_kernel, owners), out_shape=(jax.S...  69.3 us
    unnamed x14, local copies, waits for them, and re-layouts  7.22 us

profile of v3, /device:TPU:0, one launch (start us, length us, event | category | flops | bytes accessed | tf_op | source)
XLA Modules:
  0.0 77.2 jit_solution(7269824310516451042)
XLA Ops:
  0.6 0.0 copy-start
  0.6 1.8 %copy-done = bf16[4,7,192,192]{3,2,1,0:T(8,128)(2,1)S(1)} copy-done((bf16[4,7,192,192]{3,2,1,0:T(8,128)(2,1)S(1)}, bf16[4,7,192,192]{3,2,1,0:T(8,128)(2,1)}, u32[]{:S(2)}) %copy-start) | copy-done | bytes 2064408
  2.4 0.0 copy-start.1
  2.4 1.0 %copy-done.1 = bf16[2048,128]{1,0:T(8,128)(2,1)S(1)} copy-done((bf16[2048,128]{1,0:T(8,128)(2,1)S(1)}, bf16[2048,128]{1,0:T(8,128)(2,1)}, u32[]{:S(2)}) %copy-start.1) | copy-done | bytes 524312
  3.5 0.0 copy-start.2
  3.5 0.9 %copy-done.2 = bf16[128,768]{1,0:T(8,128)(2,1)S(1)} copy-done((bf16[128,768]{1,0:T(8,128)(2,1)S(1)}, bf16[128,768]{1,0:T(8,128)(2,1)}, u32[]{:S(2)}) %copy-start.2) | copy-done | bytes 196632
  4.4 0.0 copy-start.3
  4.4 0.7 copy-done.3
  5.1 0.0 copy-start.4
  5.1 0.7 copy-done.4
  5.7 0.0 copy-start.5
  5.7 0.7 copy-done.5
  6.4 69.3 %shard_map.77 = (bf16[128,768]{1,0:T(8,128)(2,1)S(1)}, bf16[144,2048]{1,0:T(8,128)(2,1)S(1)}) custom-call(bf16[128,768]{1,0:T(8,128)(2,1)S(1)} %copy-done.2, bf16[4,7,192,192]{3,2,1,0:T(8,128)(2,1)S(1)} %copy-done, s32[4,6]{1,0:T(4,128)S(1)} %copy-done.3, s32[4]{0:T(128)S(1)} %copy-done.4, s32[16]{0:T(128)S(1)} %copy-done.5, bf16[2048,128]{1,0:T(8,128)(2,1)S(1)} %copy-done.1), custom_call_target="tpu_custom_call" | custom-call | flops 2415919104 | bytes 200000000 | tf_op jit(solution)/shard_map/pallas_call | solution.py:450
  75.7 0.7 copy.10
  76.4 0.8 %copy.11 = bf16[144,2048]{1,0:T(8,128)(2,1)} copy(bf16[144,2048]{1,0:T(8,128)(2,1)S(1)} %get-tuple-element.5) | data formatting | bytes 1179648
Async XLA Ops:
  0.6 1.8 %copy-start = (bf16[4,7,192,192]{3,2,1,0:T(8,128)(2,1)S(1)}, bf16[4,7,192,192]{3,2,1,0:T(8,128)(2,1)}, u32[]{:S(2)}) copy-start(bf16[4,7,192,192]{3,2,1,0:T(8,128)(2,1)} %ham_ref.1) | copy-start | bytes 6193156
  2.4 1.0 %copy-start.1 = (bf16[2048,128]{1,0:T(8,128)(2,1)S(1)}, bf16[2048,128]{1,0:T(8,128)(2,1)}, u32[]{:S(2)}) copy-start(bf16[2048,128]{1,0:T(8,128)(2,1)} %rotation_ref.1) | copy-start | bytes 1572868
  3.5 0.9 %copy-start.2 = (bf16[128,768]{1,0:T(8,128)(2,1)S(1)}, bf16[128,768]{1,0:T(8,128)(2,1)}, u32[]{:S(2)}) copy-start(bf16[128,768]{1,0:T(8,128)(2,1)} %start_ref.1) | copy-start | bytes 589828
  4.4 0.7 copy-start.3
  5.1 0.7 copy-start.4
  5.7 0.7 copy-start.5

commit v4 on v1

--- a/solution.py
+++ b/solution.py
@@ -350,7 +350,11 @@
         advance(0, 1, False)
         return carry
 
-    lax.fori_loop(0, (DEGREE - 2) // 2, two_steps, 0)
+    split = (DEGREE - 2) // 4
+    lax.fori_loop(0, split, two_steps, 0)
+    for step in range(early + 1, chips - 1):
+        ring(step)
+    lax.fori_loop(split, (DEGREE - 2) // 2, two_steps, 0)
     advance(1, 0, False)
 
     back = pltpu.make_async_remote_copy(
@@ -362,8 +366,6 @@
         device_id_type=pl.DeviceIdType.MESH,
     )
     back.start()
-    for step in range(early + 1, chips - 1):
-        ring(step)
     masked[own_half, :] = bands[0, :, own_cols]
     back.wait()
     masked[other_half, :] = swapped[...]

time: 75.9 us -> 78.2 us (1.030)
  Pallas kernels: 67.5 us -> 70.1 us
    pallas_call x1, Pallas kernels: 67.5 us -> 70.1 us  [per_device_pair(): pl.pallas_call(functools.partial(filter_kernel, owners), out_shape=(jax.S...]
where the time goes in v4:
time: 78.2 us; the launch traced here: 78 us
  Pallas kernels  70.1 us (90%)
  local copies, waits for them, and re-layouts  7.22 us (9%)
    pallas_call x1, Pallas kernels, per_device_pair(): pl.pallas_call(functools.partial(filter_kernel, owners), out_shape=(jax.S...  70.1 us
    unnamed x14, local copies, waits for them, and re-layouts  7.22 us

profile of v4, /device:TPU:0, one launch (start us, length us, event | category | flops | bytes accessed | tf_op | source)
XLA Modules:
  0.0 78.0 jit_solution(14519338164613921490)
XLA Ops:
  0.6 0.0 copy-start
  0.6 1.8 %copy-done = bf16[4,7,192,192]{3,2,1,0:T(8,128)(2,1)S(1)} copy-done((bf16[4,7,192,192]{3,2,1,0:T(8,128)(2,1)S(1)}, bf16[4,7,192,192]{3,2,1,0:T(8,128)(2,1)}, u32[]{:S(2)}) %copy-start) | copy-done | bytes 2064408
  2.4 0.0 copy-start.1
  2.4 1.0 %copy-done.1 = bf16[2048,128]{1,0:T(8,128)(2,1)S(1)} copy-done((bf16[2048,128]{1,0:T(8,128)(2,1)S(1)}, bf16[2048,128]{1,0:T(8,128)(2,1)}, u32[]{:S(2)}) %copy-start.1) | copy-done | bytes 524312
  3.5 0.0 copy-start.2
  3.5 0.9 %copy-done.2 = bf16[128,768]{1,0:T(8,128)(2,1)S(1)} copy-done((bf16[128,768]{1,0:T(8,128)(2,1)S(1)}, bf16[128,768]{1,0:T(8,128)(2,1)}, u32[]{:S(2)}) %copy-start.2) | copy-done | bytes 196632
  4.4 0.0 copy-start.3
  4.4 0.7 copy-done.3
  5.1 0.0 copy-start.4
  5.1 0.7 copy-done.4
  5.7 0.0 copy-start.5
  5.7 0.7 copy-done.5
  6.4 70.1 %shard_map.77 = (bf16[128,768]{1,0:T(8,128)(2,1)S(1)}, bf16[144,2048]{1,0:T(8,128)(2,1)S(1)}) custom-call(bf16[128,768]{1,0:T(8,128)(2,1)S(1)} %copy-done.2, bf16[4,7,192,192]{3,2,1,0:T(8,128)(2,1)S(1)} %copy-done, s32[4,6]{1,0:T(4,128)S(1)} %copy-done.3, s32[4]{0:T(128)S(1)} %copy-done.4, s32[16]{0:T(128)S(1)} %copy-done.5, bf16[2048,128]{1,0:T(8,128)(2,1)S(1)} %copy-done.1), custom_call_target="tpu_custom_call" | custom-call | flops 2415919104 | bytes 200000000 | tf_op jit(solution)/shard_map/pallas_call | solution.py:446
  76.5 0.7 copy.10
  77.1 0.8 %copy.11 = bf16[144,2048]{1,0:T(8,128)(2,1)} copy(bf16[144,2048]{1,0:T(8,128)(2,1)S(1)} %get-tuple-element.5) | data formatting | bytes 1179648
Async XLA Ops:
  0.6 1.8 %copy-start = (bf16[4,7,192,192]{3,2,1,0:T(8,128)(2,1)S(1)}, bf16[4,7,192,192]{3,2,1,0:T(8,128)(2,1)}, u32[]{:S(2)}) copy-start(bf16[4,7,192,192]{3,2,1,0:T(8,128)(2,1)} %ham_ref.1) | copy-start | bytes 6193156
  2.4 1.0 %copy-start.1 = (bf16[2048,128]{1,0:T(8,128)(2,1)S(1)}, bf16[2048,128]{1,0:T(8,128)(2,1)}, u32[]{:S(2)}) copy-start(bf16[2048,128]{1,0:T(8,128)(2,1)} %rotation_ref.1) | copy-start | bytes 1572868
  3.5 0.9 %copy-start.2 = (bf16[128,768]{1,0:T(8,128)(2,1)S(1)}, bf16[128,768]{1,0:T(8,128)(2,1)}, u32[]{:S(2)}) copy-start(bf16[128,768]{1,0:T(8,128)(2,1)} %start_ref.1) | copy-start | bytes 589828
  4.4 0.7 copy-start.3
  5.1 0.7 copy-start.4
  5.7 0.7 copy-start.5
